TPU v7x, 32 devices: a whole 2x2x4 slice. The times are simulated.
32 devices in a mesh: grp: 2 (over x), stn: 8 (over z, y), chan: 2 (over core).
Axes of the slice: x: 2, y: 2, z: 4, core: 2. Of those that a mesh axis runs over, the one named last changes fastest.
Arguments:
- voltage: bfloat16 [2, 32, 1048576], P(None, ('grp', 'stn'), 'chan'), parts along dimension 1, may hold values from -6 to 6
- earlier_samples: bfloat16 [2, 32, 61440], P(None, ('grp', 'stn')), parts along dimension 1, may hold values from -6 to 6
- prototype: float32 [16, 4096], replicated, may hold values from -1.5 to 1.5
Outputs:
- visibilities: float32 [2, 8192, 256], P(None, ('grp', 'stn', 'chan')), parts along dimension 1
There are 2 independent parts, one for each index of `grp`. A program takes and returns all parts, laid end to end along the dimension named above; an argument that names none is the same for every part. Nothing has to cross between parts.
All inputs are finite; a program needn't handle non-finite values.
Results may differ from a plain program's by a relative error of at most 0.0044.
Values may be sent and summed in bfloat16 or wider, within the bound.
A program may use at most 64 MiB of HBM per device.

v0:
```python
import math

import jax
import jax.numpy as jnp
from jax import lax
from jax.sharding import PartitionSpec as P

FA = 64


def passed_along(block, axis, distance):
    devices = range(lax.axis_size(axis))
    route = [(i - distance, i) for i in devices if i - distance in devices]
    return lax.ppermute(block, axis, route)


def small_tables(length):
    row_index = lax.broadcasted_iota(jnp.int32, (length, length), 0)
    col_index = lax.broadcasted_iota(jnp.int32, (length, length), 1)
    phase_angle = (row_index * col_index % length).astype(jnp.float32) * (2.0 * math.pi / length)
    return (jnp.cos(phase_angle).astype(jnp.bfloat16), jnp.sin(phase_angle).astype(jnp.bfloat16))


def shards(voltage, earlier_samples, prototype):
    components, local_inputs, samples = voltage.shape
    tap_count, channels = prototype.shape
    spectra_here = samples // channels
    frames = voltage.reshape(components, local_inputs, spectra_here, channels)
    tail_frames = frames[:, :, spectra_here - (tap_count - 1) :]
    passed = passed_along(tail_frames, "chan", 1)
    earlier = earlier_samples.reshape(components, local_inputs, tap_count - 1, channels)
    leading = lax.axis_index("chan") == 0
    history = jnp.where(leading, earlier, passed)
    stacked = jnp.concatenate([history, frames], axis=2)
    filtered = jnp.zeros((components, local_inputs, spectra_here, channels), jnp.float32)
    for tap_number in range(tap_count):
        window_frames = stacked[:, :, tap_number : tap_number + spectra_here].astype(jnp.float32)
        filtered = filtered + prototype[tap_number] * window_frames
    half_rows = local_inputs * spectra_here
    first_factor = FA
    second_factor = channels // first_factor
    factored = filtered.astype(jnp.bfloat16).reshape(
        components, half_rows, first_factor, second_factor
    )
    first_cos, first_sin = small_tables(first_factor)
    second_cos, second_sin = small_tables(second_factor)
    with_cos = jnp.einsum("crab,ak->crkb", factored, first_cos, preferred_element_type=jnp.float32)
    with_sin = jnp.einsum("crab,ak->crkb", factored, first_sin, preferred_element_type=jnp.float32)
    g_real = with_cos[0] + with_sin[1]
    g_imag = with_cos[1] - with_sin[0]
    row_k = lax.broadcasted_iota(jnp.int32, (first_factor, second_factor), 0)
    col_b = lax.broadcasted_iota(jnp.int32, (first_factor, second_factor), 1)
    twist = (row_k * col_b % channels).astype(jnp.float32) * (2.0 * math.pi / channels)
    twist_cos = jnp.cos(twist)
    twist_sin = jnp.sin(twist)
    inner = jnp.stack(
        [g_real * twist_cos + g_imag * twist_sin, g_imag * twist_cos - g_real * twist_sin]
    ).astype(jnp.bfloat16)
    second_a = jnp.einsum("crkb,bm->crkm", inner, second_cos, preferred_element_type=jnp.float32)
    second_b = jnp.einsum("crkb,bm->crkm", inner, second_sin, preferred_element_type=jnp.float32)
    scale_factor = channels ** (-0.5)
    real_part = (second_a[0] + second_b[1]) * scale_factor
    imag_part = (second_a[1] - second_b[0]) * scale_factor
    ordered = jnp.transpose(jnp.stack([real_part, imag_part]), (0, 1, 3, 2))
    spectra = ordered.astype(jnp.bfloat16).reshape(components, local_inputs, spectra_here, channels)
    station_count = lax.axis_size("stn")
    core_count = lax.axis_size("chan")
    owners = station_count * core_count
    owned = channels // owners
    shaped = spectra.reshape(components, local_inputs, spectra_here, owners, owned)
    moved = lax.all_to_all(shaped, ("stn", "chan"), split_axis=3, concat_axis=3, tiled=True)
    moved = moved.reshape(components, local_inputs, spectra_here, station_count, core_count, owned)
    moved = jnp.transpose(moved, (0, 3, 1, 4, 2, 5)).reshape(
        components, station_count * local_inputs, core_count * spectra_here, owned
    )
    all_inputs = moved.shape[1]
    spectra_total = moved.shape[2]
    products = jnp.einsum("xisc,yjsc->xycij", moved, moved, preferred_element_type=jnp.float32)
    real_sum = products[0, 0] + products[1, 1]
    imag_sum = products[1, 0] - products[0, 1]
    averaged = jnp.stack([real_sum, imag_sum]) / spectra_total
    return averaged.reshape(components, owned, all_inputs * all_inputs)


def solution(mesh):
    in_specs = (P(None, ("grp", "stn"), "chan"), P(None, ("grp", "stn"), None), P())
    out_specs = P(None, ("grp", "stn", "chan"), None)
    return jax.shard_map(shards, mesh=mesh, in_specs=in_specs, out_specs=out_specs, check_vma=False)
```

profile of v0, /device:TPU:0, one launch (start us, length us, event | category | flops | bytes accessed | tf_op | source)
XLA Modules:
  0.0 261.8 jit_solution(16261250131941861124)
XLA Ops:
  0.0 0.0 copy-start.2
  0.0 0.0 copy-start.1
  0.0 7.0 %reshape.101 = bf16[2,2,128,4096]{3,2,1,0:T(8,128)(2,1)} reshape(bf16[2,2,524288]{2,1,0:T(2,128)(2,1)} %param.3) | data formatting | bytes 8388608 | tf_op jit(solution)/shard_map/reshape | solution.py:28
  7.0 1.2 slice.176
  8.2 2.4 collective-permute-start
  10.6 0.0 copy-done.2
  10.6 0.2 fusion.65
  10.8 0.0 copy-done.1
  10.8 0.3 reshape.100
  11.2 0.1 fusion.43
  11.3 0.7 collective-permute-done
  12.1 0.1 broadcast_select_fusion
  12.1 44.5 %add_convert_fusion = bf16[2,2,128,4096]{3,2,1,0:T(8,128)(2,1)} fusion(bf16[2,2,128,4096]{3,2,1,0:T(8,128)(2,1)} %reshape.101, bf16[2,2,15,4096]{3,2,1,0:T(8,128)(2,1)S(1)} %broadcast_select_fusion, f32[4096]{0:T(1024)S(1)} %bitcast.78, f32[4096]{0:T(1024)S(1)} %bitcast.79, f32[4096]{0:T(1024)S(1)} %bitcast.65, f32[4096]{0:T(1024)S(1)} %bitcast.66, ...), kind=kLoop, calls=%fused_computation.14 | loop fusion | flops 195035136 | bytes 9142272 | tf_op jit(solution)/shard_map/convert_element_type | solution.py:42
  56.6 12.6 %reshape.109 = bf16[2,256,64,64]{3,2,1,0:T(8,128)(2,1)} reshape(bf16[2,2,128,4096]{3,2,1,0:T(8,128)(2,1)} %add_convert_fusion) | data formatting | bytes 8388608 | tf_op jit(solution)/shard_map/reshape | solution.py:42
  69.2 13.5 %copy.18 = bf16[2,256,64,64]{1,2,3,0:T(8,128)(2,1)} copy(bf16[2,256,64,64]{3,2,1,0:T(8,128)(2,1)} %reshape.109) | data formatting | bytes 8388608 | tf_op jit(solution)/shard_map/reshape | solution.py:42
  82.8 0.0 copy-start
  82.8 3.7 %convolution_bitcast_fusion = f32[2,256,64,64]{1,2,3,0:T(8,128)S(1)} fusion(bf16[2,256,64,64]{1,2,3,0:T(8,128)(2,1)} %copy.18), kind=kOutput, calls=%fused_computation.58 | convolution fusion | flops 268496896 | bytes 12582912 | tf_op jit(solution)/shard_map/crab,ak->crkb/dot_general | solution.py:48
  86.5 0.0 copy-done
  86.5 1.3 convolution_bitcast_fusion.1
  87.8 2.0 add_convert_fusion.1
  89.8 0.4 pad_maximum_fusion.1
  90.2 3.4 %fusion.21 = f32[2,256,64,64]{1,3,2,0:T(8,128)S(1)} fusion(bf16[2,256,64,64]{1,2,3,0:T(8,128)(2,1)S(1)} %pad_maximum_fusion.1), kind=kOutput, calls=%fused_computation.53 | convolution fusion | flops 268496896 | bytes 12582912 | tf_op jit(solution)/shard_map/crkb,bm->crkm/dot_general | solution.py:59
  93.7 3.5 %fusion.23 = f32[2,256,64,64]{1,3,2,0:T(8,128)S(1)} fusion(bf16[2,256,64,64]{1,2,3,0:T(8,128)(2,1)S(1)} %pad_maximum_fusion.1), kind=kOutput, calls=%fused_computation.55 | convolution fusion | flops 268496896 | bytes 12582912 | tf_op jit(solution)/shard_map/crkb,bm->crkm/dot_general | solution.py:60
  97.1 2.2 fusion.17
  99.3 0.4 maximum_bitcast_fusion
  99.7 4.4 %copy.22 = bf16[2,256,64,64]{1,3,2,0:T(8,128)(2,1)} copy(bf16[2,256,64,64]{1,2,3,0:T(8,128)(2,1)S(1)} %maximum_bitcast_fusion) | data formatting | bytes 8388608 | tf_op jit(solution)/shard_map/convert_element_type | solution.py:65
  104.1 7.0 %reshape_reshape.3 = bf16[2,2,128,16,256]{2,1,4,3,0:T(2,128)(2,1)} reshape(bf16[2,256,64,64]{1,3,2,0:T(8,128)(2,1)} %copy.22) | data formatting | bytes 8388608 | tf_op jit(solution)/shard_map/reshape;reshape | solution.py:70
  111.0 5.6 %copy.23 = bf16[2,2,128,16,256]{2,1,4,0,3:T(2,128)(2,1)S(1)} copy(bf16[2,2,128,16,256]{2,1,4,3,0:T(2,128)(2,1)} %reshape_reshape.3) | data formatting | bytes 8388608 | tf_op jit(solution)/shard_map/reshape;reshape | solution.py:70
  116.6 99.0 %all_to_all.5 = bf16[2,2,128,16,256]{2,1,4,0,3:T(2,128)(2,1)} all-to-all(bf16[2,2,128,16,256]{2,1,4,0,3:T(2,128)(2,1)S(1)} %copy.23), channel_id=1, replica_groups=mesh['grp'=2,'stn'=8,'chan'=2] {'stn','chan'}, dimensions={3} | all-to-all | bytes 8388608 | tf_op jit(solution)/shard_map/all_to_all | solution.py:71
  215.6 11.1 %copy.24 = bf16[2,2,128,16,256]{4,2,3,1,0:T(8,128)(2,1)} copy(bf16[2,2,128,16,256]{2,1,4,0,3:T(2,128)(2,1)} %all_to_all.5) | data formatting | bytes 8388608 | tf_op jit(solution)/shard_map/all_to_all | solution.py:71
  226.7 11.2 %copy.25 = bf16[2,8,2,2,128,256]{4,3,2,1,0,5:T(2,128)(2,1)} copy(bf16[2,8,2,2,128,256]{5,4,3,1,2,0:T(8,128)(2,1)} %bitcast.61) | data formatting | bytes 8388608 | tf_op jit(solution)/shard_map/transpose | solution.py:73
  237.9 7.6 %reshape.107 = bf16[2,16,256,256,1]{2,1,0,3,4:T(8,128)(2,1)} reshape(bf16[2,8,2,2,128,256]{4,3,2,1,0,5:T(2,128)(2,1)} %copy.25) | data formatting | bytes 8388608 | tf_op jit(solution)/shard_map/reshape | solution.py:73
  245.5 9.7 %fusion.25 = f32[2,2,256,16,16]{3,4,0,1,2:T(8,128)S(1)} fusion(bf16[2,16,256,256,1]{2,1,0,3,4:T(8,128)(2,1)} %reshape.107), kind=kOutput, calls=%fused_computation.57 | convolution fusion | flops 134217728 | bytes 5242880 | tf_op jit(solution)/shard_map/xisc,yjsc->xycij/dot_general | solution.py:78
  255.2 1.9 slice_add_fusion.2
  257.1 2.6 copy.26
  259.7 1.1 copy.27
  260.8 1.0 copy.28
  (1 shorter events, 0.0 us)
Async XLA Ops:
  0.0 10.6 %copy-start.2 = (f32[16,4096]{1,0:T(8,128)S(1)}, f32[16,4096]{1,0:T(8,128)}, u32[]{:S(2)}) copy-start(f32[16,4096]{1,0:T(8,128)} %param.5) | copy-start | bytes 786436
  0.0 10.8 %copy-start.1 = (bf16[2,2,61440]{2,1,0:T(2,128)(2,1)S(1)}, bf16[2,2,61440]{2,1,0:T(2,128)(2,1)}, u32[]{:S(2)}) copy-start(bf16[2,2,61440]{2,1,0:T(2,128)(2,1)} %param.4) | copy-start | bytes 1474564
  8.2 3.9 %collective-permute-start = (bf16[2,2,15,4096]{3,2,1,0:T(8,128)(2,1)S(1)}, bf16[2,2,15,4096]{3,2,1,0:T(8,128)(2,1)S(1)}, u32[]{:S(2)}, u32[]{:S(2)}) collective-permute-start(bf16[2,2,15,4096]{3,2,1,0:T(8,128)(2,1)S(1)} %slice.176), channel_id=1, source_target_pairs={{0,1},{2,3},{4,5},{6,7},{8,9},{10,11},{12,13},{14,15},{16,17},{18,... | collective-permute-start | bytes 1474568 | tf_op jit(solution)/shard_map/ppermute | solution.py:14
  82.8 3.7 %copy-start = (bf16[2,256,64,64]{1,2,3,0:T(8,128)(2,1)S(1)}, bf16[2,256,64,64]{1,2,3,0:T(8,128)(2,1)}, u32[]{:S(2)}) copy-start(bf16[2,256,64,64]{1,2,3,0:T(8,128)(2,1)} %copy.18) | copy-start | bytes 12582916
where the time goes:
time: 264 us; the launch traced here: 262 us
  blocking collectives  99 us (38%)
  local copies, waits for them, and re-layouts  86.4 us (33%)
  other arithmetic  51.5 us (20%)
  matrix products  21.6 us (8%)
    all_to_all x1, blocking collectives, shards(): lax.all_to_all(shaped, ('stn', 'chan'), split_axis=3, concat_axis=3, tile...  99 us
    convert_element_type x1, other arithmetic, shards(): filtered.astype(jnp.bfloat16)  44.5 us
    reshape x2, local copies, waits for them, and re-layouts, shards(): filtered.astype(jnp.bfloat16)  26.2 us
    another operation x2, local copies, waits for them, and re-layouts, shards(): spectra.reshape(components, local_inputs, spectra_here, owners, owned)  12.5 us
    transpose x1, local copies, waits for them, and re-layouts, shards(): jnp.transpose(moved, (0, 3, 1, 4, 2, 5))  11.2 us
    all_to_all x1, local copies, waits for them, and re-layouts, shards(): lax.all_to_all(shaped, ('stn', 'chan'), split_axis=3, concat_axis=3, tile...  11.1 us
    dot_general x1, matrix products, shards(): jnp.einsum('xisc,yjsc->xycij', moved, moved, preferred_element_type=jnp.f...  9.68 us
    reshape x1, local copies, waits for them, and re-layouts, shards(): jnp.transpose(moved, (0, 3, 1, 4, 2, 5))  7.59 us
  transfers between devices with their start and end apart: 1, of which 1 were waited for; matrix products, arithmetic and copies ran while one was open for 0% of the time, Pallas kernels for 0%

commit v1 on v0

--- a/solution.py
+++ b/solution.py
@@ -1,11 +1,20 @@
+import functools
 import math
 
 import jax
 import jax.numpy as jnp
+import numpy as np
 from jax import lax
+from jax.experimental import pallas as pl
+from jax.experimental.pallas import tpu as pltpu
 from jax.sharding import PartitionSpec as P
 
 FA = 64
+LANES = 128
+SUB = 8
+PACK = 16
+GROUPS = 4
+MESH = pl.DeviceIdType.MESH
 
 
 def passed_along(block, axis, distance):
@@ -21,7 +30,7 @@
     return (jnp.cos(phase_angle).astype(jnp.bfloat16), jnp.sin(phase_angle).astype(jnp.bfloat16))
 
 
-def shards(voltage, earlier_samples, prototype):
+def general_shards(voltage, earlier_samples, prototype):
     components, local_inputs, samples = voltage.shape
     tap_count, channels = prototype.shape
     spectra_here = samples // channels
@@ -82,6 +91,268 @@
     return averaged.reshape(components, owned, all_inputs * all_inputs)
 
 
+def tables(channels, owners, rows, inputs):
+    q_count = channels // LANES
+    q = np.arange(q_count)
+    lane = np.arange(LANES)
+    ang1 = 2.0 * np.pi * (np.outer(q, q) % q_count) / q_count
+    cos1, sin1 = np.cos(ang1), np.sin(ang1)
+    one = np.block([[cos1, sin1], [-sin1, cos1]])
+    one = one.reshape(2, q_count, 2, q_count)
+    eye = np.eye(SUB)
+    first = np.einsum("ckdq,st->ckstdq", one, eye).reshape(2 * q_count * SUB, SUB * 2 * q_count)
+    ang = 2.0 * np.pi * (np.outer(q, lane) % channels) / channels
+    twist_cos, twist_sin = np.cos(ang), np.sin(ang)
+    ang2 = 2.0 * np.pi * (np.outer(lane, lane) % LANES) / LANES
+    scale = channels ** -0.5
+    cos2, sin2 = np.cos(ang2) * scale, np.sin(ang2) * scale
+    two = np.stack([np.stack([cos2, sin2], 1), np.stack([-sin2, cos2], 1)])
+    two = two.reshape(2, owners, rows, 2, LANES).transpose(1, 0, 2, 3, 4)
+    second = two.reshape(2 * LANES, 2 * LANES)
+    pick = np.einsum("ia,jb->ijab", np.eye(inputs), np.eye(inputs))
+    pick = np.repeat(pick[:, :, None], rows, axis=2)
+    pick = pick.reshape(inputs * inputs * rows, inputs * inputs)
+    return (
+        jnp.asarray(first, jnp.bfloat16),
+        jnp.asarray(twist_cos, jnp.float32),
+        jnp.asarray(twist_sin, jnp.float32),
+        jnp.asarray(second, jnp.bfloat16),
+        jnp.asarray(pick, jnp.bfloat16),
+    )
+
+
+def correlator(
+    stations, cores, stacked, proto, first, twist_cos, twist_sin, second, pick, out,
+    held, inner, spec, recv, panel, send_sem, recv_sem, own_sem,
+):
+    owners = stations * cores
+    local_inputs = stacked.shape[1]
+    tap_count, q_count = proto.shape[:2]
+    blocks = held.shape[0]
+    spectra_here = blocks * SUB
+    inputs = stations * local_inputs
+    per_group = q_count // GROUPS
+    stn, core = lax.axis_index("stn"), lax.axis_index("chan")
+    me = stn * cores + core
+
+    barrier = pltpu.get_barrier_semaphore()
+
+    def greet(r, carry):
+        peer = lax.rem(me + r, owners)
+        pl.semaphore_signal(
+            barrier, inc=1, device_id={"stn": peer // cores, "chan": lax.rem(peer, cores)},
+            device_id_type=MESH,
+        )
+        return carry
+
+    lax.fori_loop(1, owners, greet, 0)
+
+    def copy_out(i, group, peer):
+        part = pl.ds(group * per_group, per_group)
+        return pltpu.make_async_remote_copy(
+            src_ref=spec.at[i, peer, part],
+            dst_ref=recv.at[core, stn * local_inputs + i, part],
+            send_sem=send_sem.at[i, group, peer],
+            recv_sem=recv_sem.at[i, group, me],
+            device_id={"stn": peer // cores, "chan": lax.rem(peer, cores)},
+            device_id_type=MESH,
+        )
+
+    def copy_in(i, group, peer):
+        part = pl.ds(group * per_group, per_group)
+        return pltpu.make_async_remote_copy(
+            src_ref=spec.at[i, peer, part],
+            dst_ref=recv.at[lax.rem(peer, cores), peer // cores * local_inputs + i, part],
+            send_sem=send_sem.at[i, group, peer],
+            recv_sem=recv_sem.at[i, group, peer],
+            device_id={"stn": peer // cores, "chan": lax.rem(peer, cores)},
+            device_id_type=MESH,
+        )
+
+    def copy_own(i, group):
+        part = pl.ds(group * per_group, per_group)
+        return pltpu.make_async_copy(
+            spec.at[i, me, part], recv.at[core, stn * local_inputs + i, part], own_sem.at[i, group]
+        )
+
+    halves = q_count // PACK
+    for i in range(local_inputs):
+
+        def filter_block(n, carry):
+            block = n // (2 * halves)
+            c = lax.rem(n // halves, 2)
+            rows = pl.ds(pl.multiple_of(lax.rem(n, halves) * PACK, PACK), PACK)
+            sums = [None] * SUB
+            for f in range(SUB + tap_count - 1):
+                frame = stacked[c, i, block * SUB + f, rows, :].astype(jnp.float32)
+                for s in range(max(0, f - tap_count + 1), min(SUB, f + 1)):
+                    term = proto[f - s, rows, :] * frame
+                    sums[s] = term if sums[s] is None else sums[s] + term
+            for s in range(SUB):
+                held[block, s, c, rows, :] = sums[s].astype(jnp.bfloat16)
+            return carry
+
+        lax.fori_loop(0, blocks * 2 * halves, filter_block, 0)
+
+        def first_stage(pair, carry):
+            wide = SUB * 2 * q_count
+            x = jnp.concatenate(
+                [held[2 * pair].reshape(wide, LANES), held[2 * pair + 1].reshape(wide, LANES)], axis=1
+            )
+            g = jnp.dot(first[...], x, preferred_element_type=jnp.float32)
+            g = g.reshape(2, q_count, SUB, 2 * LANES)
+            g = jnp.concatenate([g[..., :LANES], g[..., LANES:]], axis=2)
+            cos = twist_cos[...][:, None, :]
+            sin = twist_sin[...][:, None, :]
+            rows = pl.ds(pl.multiple_of(pair * PACK, PACK), PACK)
+            inner[:, rows, pl.ds(0, LANES)] = (g[0] * cos + g[1] * sin).astype(jnp.bfloat16)
+            inner[:, rows, pl.ds(LANES, LANES)] = (g[1] * cos - g[0] * sin).astype(jnp.bfloat16)
+            return carry
+
+        lax.fori_loop(0, blocks // 2, first_stage, 0)
+
+        if i == 0:
+            pl.semaphore_wait(barrier, owners - 1)
+
+        def second_stage(group, carry):
+            def one_pair(n, inside):
+                k = group * per_group + 2 * n
+                z = inner[pl.ds(k, 2)].reshape(2 * spectra_here, 2 * LANES)
+                made = lax.dot_general(
+                    second[...], z, (((1,), (1,)), ((), ())), preferred_element_type=jnp.float32
+                ).astype(jnp.bfloat16)
+                for e in range(2):
+                    piece = made[:, e * spectra_here : (e + 1) * spectra_here]
+                    spec[i, :, k + e] = piece.reshape(owners, PACK, spectra_here)
+                return inside
+
+            lax.fori_loop(0, per_group // 2, one_pair, 0)
+
+            def send(r, inside):
+                side = 1 - 2 * lax.rem(r, 2)
+                peer = lax.rem(me + owners // 2 + side * ((r + 1) // 2) + owners, owners)
+                copy_out(i, group, peer).start()
+                return inside
+
+            lax.fori_loop(0, owners - 1, send, 0)
+            copy_own(i, group).start()
+            return carry
+
+        lax.fori_loop(0, GROUPS, second_stage, 0)
+
+    row = lax.broadcasted_iota(jnp.int32, (SUB, LANES), 0)
+    col = lax.broadcasted_iota(jnp.int32, (SUB, LANES), 1)
+    same = (lax.rem(col, SUB) == row).astype(jnp.float32) * (1.0 / (cores * spectra_here))
+
+    def correlate(group, carry):
+        for i in range(local_inputs):
+
+            def arrived(r, inside):
+                copy_in(i, group, lax.rem(me + r, owners)).wait_recv()
+                return inside
+
+            lax.fori_loop(1, owners, arrived, 0)
+            copy_own(i, group).wait()
+
+        def one(n, inside):
+            k = group * per_group + n
+            left, right = [], []
+            for h in range(cores):
+                a = recv[h, :, k].astype(jnp.float32).reshape(inputs, 2, SUB, spectra_here)
+                re = a[:, 0].reshape(inputs * SUB, spectra_here)
+                im = a[:, 1].reshape(inputs * SUB, spectra_here)
+                left.append(jnp.concatenate([re, im], axis=0).astype(jnp.bfloat16))
+                left.append(jnp.concatenate([im, -re], axis=0).astype(jnp.bfloat16))
+                right.append(re.astype(jnp.bfloat16))
+                right.append(im.astype(jnp.bfloat16))
+            v = lax.dot_general(
+                jnp.concatenate(left, axis=1), jnp.concatenate(right, axis=1),
+                (((1,), (1,)), ((), ())), preferred_element_type=jnp.float32,
+            ).reshape(2, inputs, SUB, LANES)
+            for c in range(2):
+                for j in range(inputs):
+                    panel[c, n, :, pl.ds(j * LANES, LANES)] = v[c, j] * same
+            return inside
+
+        lax.fori_loop(0, per_group, one, 0)
+        flat = panel[...].reshape(2 * per_group * SUB, inputs * LANES)
+        high = flat.astype(jnp.bfloat16)
+        low = (flat - high.astype(jnp.float32)).astype(jnp.bfloat16)
+        total = jnp.dot(high, pick[...], preferred_element_type=jnp.float32) + jnp.dot(
+            low, pick[...], preferred_element_type=jnp.float32
+        )
+        total = total.reshape(2, per_group, SUB, inputs * inputs)
+        out[:, pl.ds(group * per_group, per_group)] = total
+        return carry
+
+    lax.fori_loop(0, GROUPS, correlate, 0)
+
+    def drain(n, carry):
+        i, group, r = n // (GROUPS * (owners - 1)), lax.rem(n // (owners - 1), GROUPS), lax.rem(n, owners - 1)
+        copy_out(i, group, lax.rem(me + 1 + r, owners)).wait_send()
+        return carry
+
+    lax.fori_loop(0, local_inputs * GROUPS * (owners - 1), drain, 0)
+
+
+def kernel_fits(voltage, prototype, owners, inputs):
+    spectra_here = voltage.shape[2] // prototype.shape[1]
+    channels = prototype.shape[1]
+    return (
+        channels == 32 * LANES
+        and spectra_here == LANES
+        and channels // owners == 32 * SUB
+        and inputs * SUB == LANES
+    )
+
+
+def shards(voltage, earlier_samples, prototype):
+    components, local_inputs, samples = voltage.shape
+    tap_count, channels = prototype.shape
+    stations, cores = lax.axis_size("stn"), lax.axis_size("chan")
+    owners, inputs = stations * cores, stations * local_inputs
+    if not kernel_fits(voltage, prototype, owners, inputs):
+        return general_shards(voltage, earlier_samples, prototype)
+    spectra_here = samples // channels
+    q_count = channels // LANES
+    rows = channels // owners // q_count
+    tail = voltage[:, :, samples - (tap_count - 1) * channels :]
+    passed = passed_along(tail, "chan", 1)
+    history = jnp.where(lax.axis_index("chan") == 0, earlier_samples, passed)
+    stacked = jnp.concatenate(
+        [
+            history.reshape(components, local_inputs, tap_count - 1, q_count, LANES),
+            voltage.reshape(components, local_inputs, spectra_here, q_count, LANES),
+        ],
+        axis=2,
+    )
+    proto = prototype.reshape(tap_count, q_count, LANES)
+    consts = tables(channels, owners, rows, inputs)
+    vmem = pl.BlockSpec(memory_space=pltpu.VMEM)
+    blocks = spectra_here // SUB
+    made = pl.pallas_call(
+        functools.partial(correlator, stations, cores),
+        out_shape=jax.ShapeDtypeStruct((components, q_count, rows, inputs * inputs), jnp.float32),
+        in_specs=[vmem] * 7,
+        out_specs=vmem,
+        scratch_shapes=[
+            pltpu.VMEM((blocks, SUB, components, q_count, LANES), jnp.bfloat16),
+            pltpu.VMEM((q_count, spectra_here, 2 * LANES), jnp.bfloat16),
+            pltpu.VMEM((local_inputs, owners, q_count, PACK, spectra_here), jnp.bfloat16),
+            pltpu.VMEM((cores, inputs, q_count, PACK, spectra_here), jnp.bfloat16),
+            pltpu.VMEM((components, q_count // GROUPS, SUB, inputs * LANES), jnp.float32),
+            pltpu.SemaphoreType.DMA((local_inputs, GROUPS, owners)),
+            pltpu.SemaphoreType.DMA((local_inputs, GROUPS, owners)),
+            pltpu.SemaphoreType.DMA((local_inputs, GROUPS)),
+        ],
+        compiler_params=pltpu.CompilerParams(
+            collective_id=0, has_side_effects=True, vmem_limit_bytes=48 * 1024 * 1024
+        ),
+    )(stacked, proto, *consts)
+    made = jnp.transpose(made, (0, 2, 1, 3))
+    return made.reshape(components, rows * q_count, inputs * inputs)
+
+
 def solution(mesh):
     in_specs = (P(None, ("grp", "stn"), "chan"), P(None, ("grp", "stn"), None), P())
     out_specs = P(None, ("grp", "stn", "chan"), None)

time: 264 us -> 129 us (0.49)
  Pallas kernels: 0 us -> 112 us
  blocking collectives: 99 us -> 0 us
  local copies, waits for them, and re-layouts: 86.4 us -> 8.98 us
  other arithmetic: 51.5 us -> 5.34 us
  matrix products: 21.6 us -> 0 us
    pallas_call x0 -> x1, Pallas kernels: none -> 112 us  [shards(): pl.pallas_call(functools.partial(correlator, stations, cores), out_shape=...]
    all_to_all x1 -> x0, blocking collectives: 99 us -> none  [shards(): lax.all_to_all(shaped, ('stn', 'chan'), split_axis=3, concat_axis=3, tile...]
    convert_element_type x2 -> x0, other arithmetic: 44.9 us -> none  [the longest x1 44.5 us: shards(): filtered.astype(jnp.bfloat16)]
    reshape x5 -> x2, local copies, waits for them, and re-layouts: 41.1 us -> 6.52 us  [the longest x1 6.1 us: shards(): voltage.reshape(components, local_inputs, spectra_here, q_count, LANES)]
    dot_general x5 -> x0, matrix products: 21.6 us -> none  [the longest x1 9.68 us: shards(): jnp.einsum('xisc,yjsc->xycij', moved, moved, preferred_element_type=jnp.f...]
    another operation x2 -> x0, local copies, waits for them, and re-layouts: 12.5 us -> none  [shards(): spectra.reshape(components, local_inputs, spectra_here, owners, owned)]
    all_to_all x1 -> x0, local copies, waits for them, and re-layouts: 11.1 us -> none  [shards(): lax.all_to_all(shaped, ('stn', 'chan'), split_axis=3, concat_axis=3, tile...]
    transpose x1, local copies, waits for them, and re-layouts: 11.2 us -> 0.95 us  [shards(): made = jnp.transpose(made, (0, 2, 1, 3))]
  transfers between devices with their start and end apart: 1 -> 1, of which waited for: 1 -> 0; matrix products, arithmetic and copies ran while one was open for 0% -> 5% of each run, Pallas kernels for 0% -> 0%
where the time goes in v1:
time: 129 us
  Pallas kernels  112 us (87%)
  local copies, waits for them, and re-layouts  8.98 us (7%)
  other arithmetic  5.34 us (4%)
  starting transfers between devices  2.52 us (2%)
    pallas_call x1, Pallas kernels, shards(): pl.pallas_call(functools.partial(correlator, stations, cores), out_shape=...  112 us
    reshape x1, local copies, waits for them, and re-layouts, shards(): voltage.reshape(components, local_inputs, spectra_here, q_count, LANES)  6.1 us
    concatenate x1, other arithmetic, shards(): jnp.concatenate([history.reshape(components, local_inputs, tap_count - 1,...  4.83 us
  transfers between devices with their start and end apart: 1, of which 0 were waited for; matrix products, arithmetic and copies ran while one was open for 5% of the time, Pallas kernels for 0%

profile of v1, /device:TPU:0, one launch (start us, length us, event | category | flops | bytes accessed | tf_op | source)
XLA Modules:
  0.0 128.8 jit_solution(7718120361710519362)
XLA Ops:
  0.0 0.0 copy-start.6
  0.0 1.4 %slice.3 = bf16[2,2,61440]{2,1,0:T(2,128)(2,1)S(1)} slice(bf16[2,2,524288]{2,1,0:T(2,128)(2,1)} %param.8), slice={[0:2], [0:2], [462848:524288]} | slice | bytes 983040 | tf_op jit(solution)/shard_map/slice | solution.py:319
  1.4 0.0 copy-start.5
  1.4 2.5 %collective-permute-start = (bf16[2,2,61440]{2,1,0:T(2,128)(2,1)S(1)}, bf16[2,2,61440]{2,1,0:T(2,128)(2,1)S(1)}, u32[]{:S(2)}, u32[]{:S(2)}) collective-permute-start(bf16[2,2,61440]{2,1,0:T(2,128)(2,1)S(1)} %slice.3), channel_id=1, source_target_pairs={{0,1},{2,3},{4,5},{6,7},{8,9},{10,11},{12,13},{14,15},{16,17},{18,... | collective-permute-start | bytes 1474568 | tf_op jit(solution)/shard_map/ppermute | solution.py:23
  4.0 6.1 %reshape.13 = bf16[2,2,128,32,128]{4,3,2,1,0:T(8,128)(2,1)} reshape(bf16[2,2,524288]{2,1,0:T(2,128)(2,1)} %param.8) | data formatting | bytes 8388608 | tf_op jit(solution)/shard_map/reshape | solution.py:325
  10.1 0.0 copy-done.6
  10.1 0.1 copy.10
  10.1 0.0 collective-permute-done
  10.1 0.0 copy-done.5
  10.1 0.5 broadcast_select_fusion
  10.7 0.4 reshape.12
  11.1 0.0 copy-start
  11.1 0.0 copy-start.1
  11.1 0.0 copy-start.2
  11.1 0.0 copy-start.3
  11.1 0.0 copy-start.4
  11.2 4.8 %pad_maximum_fusion.stacked = bf16[2,2,143,32,128]{4,3,2,1,0:T(8,128)(2,1)} fusion(bf16[2,2,128,32,128]{4,3,2,1,0:T(8,128)(2,1)} %reshape.13, bf16[2,2,15,32,128]{4,3,2,1,0:T(8,128)(2,1)S(1)} %reshape.12), kind=kLoop, calls=%fused_computation | loop fusion | flops 2342912 | bytes 9371648 | tf_op jit(solution)/shard_map/concatenate | solution.py:322
  16.0 0.0 copy-done
  16.0 0.0 copy-done.1
  16.0 0.0 copy-done.2
  16.0 0.0 copy-done.3
  16.0 0.0 copy-done.4
  16.0 111.8 %shard_map.82 = f32[2,32,8,256]{3,2,1,0:T(8,128)S(1)} custom-call(bf16[2,2,143,32,128]{4,3,2,1,0:T(8,128)(2,1)} %pad_maximum_fusion.stacked, f32[16,32,128]{2,1,0:T(8,128)S(1)} %bitcast.5, bf16[512,512]{1,0:T(8,128)(2,1)S(1)} %copy-done.1, f32[32,128]{1,0:T(8,128)S(1)} %copy-done.3, f32[32,128]{1,0:T(8,128)S(1)} %copy-done.4, ...), custom_call_target="tpu_custom_call" | custom-call | tf_op jit(solution)/shard_map/pallas_call | solution.py:333
  127.8 1.0 copy.9
Async XLA Ops:
  0.0 10.1 %copy-start.6 = (f32[16,4096]{1,0:T(8,128)S(1)}, f32[16,4096]{1,0:T(8,128)}, u32[]{:S(2)}) copy-start(f32[16,4096]{1,0:T(8,128)} %param.10) | copy-start | bytes 786436
  1.4 8.7 %copy-start.5 = (bf16[2,2,61440]{2,1,0:T(2,128)(2,1)S(1)}, bf16[2,2,61440]{2,1,0:T(2,128)(2,1)}, u32[]{:S(2)}) copy-start(bf16[2,2,61440]{2,1,0:T(2,128)(2,1)} %param.9) | copy-start | bytes 1474564
  1.4 8.7 %collective-permute-start = (bf16[2,2,61440]{2,1,0:T(2,128)(2,1)S(1)}, bf16[2,2,61440]{2,1,0:T(2,128)(2,1)S(1)}, u32[]{:S(2)}, u32[]{:S(2)}) collective-permute-start(bf16[2,2,61440]{2,1,0:T(2,128)(2,1)S(1)} %slice.3), channel_id=1, source_target_pairs={{0,1},{2,3},{4,5},{6,7},{8,9},{10,11},{12,13},{14,15},{16,17},{18,... | collective-permute-start | bytes 1474568 | tf_op jit(solution)/shard_map/ppermute | solution.py:23
  11.1 4.9 %copy-start = (bf16[2048,256]{1,0:T(8,128)(2,1)S(1)}, bf16[2048,256]{1,0:T(8,128)(2,1)}, u32[]{:S(2)}) copy-start(bf16[2048,256]{1,0:T(8,128)(2,1)} %constant.20.clone.pick) | copy-start | bytes 3145732
  11.1 4.9 %copy-start.1 = (bf16[512,512]{1,0:T(8,128)(2,1)S(1)}, bf16[512,512]{1,0:T(8,128)(2,1)}, u32[]{:S(2)}) copy-start(bf16[512,512]{1,0:T(8,128)(2,1)} %constant.16.clone.first) | copy-start | bytes 1572868
  11.1 4.9 %copy-start.2 = (bf16[256,256]{1,0:T(8,128)(2,1)S(1)}, bf16[256,256]{1,0:T(8,128)(2,1)}, u32[]{:S(2)}) copy-start(bf16[256,256]{1,0:T(8,128)(2,1)} %constant.19.clone.second) | copy-start | bytes 393220
  11.1 4.9 %copy-start.3 = (f32[32,128]{1,0:T(8,128)S(1)}, f32[32,128]{1,0:T(8,128)}, u32[]{:S(2)}) copy-start(f32[32,128]{1,0:T(8,128)} %constant.17.clone.twist_cos) | copy-start | bytes 49156
  11.1 4.9 %copy-start.4 = (f32[32,128]{1,0:T(8,128)S(1)}, f32[32,128]{1,0:T(8,128)}, u32[]{:S(2)}) copy-start(f32[32,128]{1,0:T(8,128)} %constant.18.clone.twist_sin) | copy-start | bytes 49156

commit v2 on v1

--- a/solution.py
+++ b/solution.py
@@ -14,6 +14,7 @@
 SUB = 8
 PACK = 16
 GROUPS = 4
+CHUNKS = 2
 MESH = pl.DeviceIdType.MESH
 
 
@@ -100,7 +101,9 @@
     one = np.block([[cos1, sin1], [-sin1, cos1]])
     one = one.reshape(2, q_count, 2, q_count)
     eye = np.eye(SUB)
-    first = np.einsum("ckdq,st->ckstdq", one, eye).reshape(2 * q_count * SUB, SUB * 2 * q_count)
+    both = np.eye(2)
+    first = np.einsum("ckdq,st,ij->ickstdqj", one, eye, both)
+    first = first.reshape(4 * q_count * SUB, 4 * q_count * SUB)
     ang = 2.0 * np.pi * (np.outer(q, lane) % channels) / channels
     twist_cos, twist_sin = np.cos(ang), np.sin(ang)
     ang2 = 2.0 * np.pi * (np.outer(lane, lane) % LANES) / LANES
@@ -122,18 +125,21 @@
 
 
 def correlator(
-    stations, cores, stacked, proto, first, twist_cos, twist_sin, second, pick, out,
-    held, inner, spec, recv, panel, send_sem, recv_sem, own_sem,
+    stations, cores, voltage, earlier, first_hbm, pick_hbm, proto, twist_cos, twist_sin, second, out,
+    stream, first, pick, held, inner, spec, recv, panel, send_sem, recv_sem, own_sem, load_sem, halo_sem,
 ):
     owners = stations * cores
-    local_inputs = stacked.shape[1]
-    tap_count, q_count = proto.shape[:2]
+    local_inputs = 2
+    tap_count, frame_rows = proto.shape[:2]
+    q_count = frame_rows // local_inputs
     blocks = held.shape[0]
-    spectra_here = blocks * SUB
+    spectra_chunk = blocks * SUB
+    spectra_here = CHUNKS * spectra_chunk
     inputs = stations * local_inputs
     per_group = q_count // GROUPS
     stn, core = lax.axis_index("stn"), lax.axis_index("chan")
     me = stn * cores + core
+    lead = tap_count - 1
 
     barrier = pltpu.get_barrier_semaphore()
 
@@ -145,13 +151,47 @@
         )
         return carry
 
+    def load(c, begin, end, sem):
+        count = (end - begin) * frame_rows
+        return pltpu.make_async_copy(
+            voltage.at[c, pl.ds(begin * frame_rows, count)],
+            stream.at[c, pl.ds((begin + lead) * frame_rows, count)],
+            load_sem.at[sem],
+        )
+
+    split = spectra_here - spectra_chunk - lead
+    late = [load(c, split, spectra_here, c) for c in range(2)]
+    early = [load(c, 0, split, 2 + c) for c in range(2)]
+    get_first = pltpu.make_async_copy(first_hbm, first, load_sem.at[4])
+    get_pick = pltpu.make_async_copy(pick_hbm, pick, load_sem.at[5])
+    history = stream.at[:, pl.ds(0, lead * frame_rows)]
+    get_earlier = pltpu.make_async_copy(earlier, history, load_sem.at[6])
+    halo = pltpu.make_async_remote_copy(
+        src_ref=voltage.at[:, pl.ds((spectra_here - lead) * frame_rows, lead * frame_rows)],
+        dst_ref=history,
+        send_sem=halo_sem.at[0],
+        recv_sem=halo_sem.at[1],
+        device_id={"stn": stn, "chan": lax.rem(core + 1, cores)},
+        device_id_type=MESH,
+    )
+    for copy in late:
+        copy.start()
+    get_first.start()
     lax.fori_loop(1, owners, greet, 0)
+    for copy in early:
+        copy.start()
+
+    @pl.when(core == 0)
+    def _():
+        get_earlier.start()
+
+    get_pick.start()
 
     def copy_out(i, group, peer):
         part = pl.ds(group * per_group, per_group)
         return pltpu.make_async_remote_copy(
             src_ref=spec.at[i, peer, part],
-            dst_ref=recv.at[core, stn * local_inputs + i, part],
+            dst_ref=recv.at[core, i, stn, part],
             send_sem=send_sem.at[i, group, peer],
             recv_sem=recv_sem.at[i, group, me],
             device_id={"stn": peer // cores, "chan": lax.rem(peer, cores)},
@@ -162,7 +202,7 @@
         part = pl.ds(group * per_group, per_group)
         return pltpu.make_async_remote_copy(
             src_ref=spec.at[i, peer, part],
-            dst_ref=recv.at[lax.rem(peer, cores), peer // cores * local_inputs + i, part],
+            dst_ref=recv.at[lax.rem(peer, cores), i, peer // cores, part],
             send_sem=send_sem.at[i, group, peer],
             recv_sem=recv_sem.at[i, group, peer],
             device_id={"stn": peer // cores, "chan": lax.rem(peer, cores)},
@@ -172,58 +212,83 @@
     def copy_own(i, group):
         part = pl.ds(group * per_group, per_group)
         return pltpu.make_async_copy(
-            spec.at[i, me, part], recv.at[core, stn * local_inputs + i, part], own_sem.at[i, group]
-        )
-
-    halves = q_count // PACK
-    for i in range(local_inputs):
+            spec.at[i, me, part], recv.at[core, i, stn, part], own_sem.at[i, group]
+        )
+
+    pieces = frame_rows // PACK
+    for i in range(CHUNKS):
+        start = spectra_here - (i + 1) * spectra_chunk
+        if i == 0:
+            for copy in late:
+                copy.wait()
+        else:
+            for copy in early:
+                copy.wait()
+
+            @pl.when(core == 0)
+            def _():
+                get_earlier.wait()
+
+            @pl.when(core > 0)
+            def _():
+                halo.wait_recv()
 
         def filter_block(n, carry):
-            block = n // (2 * halves)
-            c = lax.rem(n // halves, 2)
-            rows = pl.ds(pl.multiple_of(lax.rem(n, halves) * PACK, PACK), PACK)
+            block = n // (2 * pieces)
+            c = lax.rem(n // pieces, 2)
+            offset = lax.rem(n, pieces) * PACK
+            rows = pl.ds(pl.multiple_of(offset, PACK), PACK)
             sums = [None] * SUB
-            for f in range(SUB + tap_count - 1):
-                frame = stacked[c, i, block * SUB + f, rows, :].astype(jnp.float32)
-                for s in range(max(0, f - tap_count + 1), min(SUB, f + 1)):
+            for f in range(SUB + lead):
+                place = (start + block * SUB + f) * frame_rows + offset
+                frame = stream[c, pl.ds(pl.multiple_of(place, PACK), PACK), :].astype(jnp.float32)
+                for s in range(max(0, f - lead), min(SUB, f + 1)):
                     term = proto[f - s, rows, :] * frame
                     sums[s] = term if sums[s] is None else sums[s] + term
             for s in range(SUB):
                 held[block, s, c, rows, :] = sums[s].astype(jnp.bfloat16)
             return carry
 
-        lax.fori_loop(0, blocks * 2 * halves, filter_block, 0)
-
-        def first_stage(pair, carry):
-            wide = SUB * 2 * q_count
+        lax.fori_loop(0, blocks * 2 * pieces, filter_block, 0)
+        if i == 0:
+            get_first.wait()
+            pl.semaphore_wait(barrier, owners - 1)
+
+            @pl.when(core < cores - 1)
+            def _():
+                halo.start()
+
+        half = 2 * q_count * SUB
+
+        def first_stage(n, carry):
+            pair, part = n // local_inputs, lax.rem(n, local_inputs)
+            wide = SUB * 2 * frame_rows
             x = jnp.concatenate(
                 [held[2 * pair].reshape(wide, LANES), held[2 * pair + 1].reshape(wide, LANES)], axis=1
             )
-            g = jnp.dot(first[...], x, preferred_element_type=jnp.float32)
+            weights = first[pl.ds(pl.multiple_of(part * half, half), half), :]
+            g = jnp.dot(weights, x, preferred_element_type=jnp.float32)
             g = g.reshape(2, q_count, SUB, 2 * LANES)
             g = jnp.concatenate([g[..., :LANES], g[..., LANES:]], axis=2)
             cos = twist_cos[...][:, None, :]
             sin = twist_sin[...][:, None, :]
-            rows = pl.ds(pl.multiple_of(pair * PACK, PACK), PACK)
+            rows = pl.ds(pl.multiple_of(part * spectra_chunk + pair * PACK, PACK), PACK)
             inner[:, rows, pl.ds(0, LANES)] = (g[0] * cos + g[1] * sin).astype(jnp.bfloat16)
             inner[:, rows, pl.ds(LANES, LANES)] = (g[1] * cos - g[0] * sin).astype(jnp.bfloat16)
             return carry
 
-        lax.fori_loop(0, blocks // 2, first_stage, 0)
-
-        if i == 0:
-            pl.semaphore_wait(barrier, owners - 1)
+        lax.fori_loop(0, blocks // 2 * local_inputs, first_stage, 0)
 
         def second_stage(group, carry):
             def one_pair(n, inside):
                 k = group * per_group + 2 * n
-                z = inner[pl.ds(k, 2)].reshape(2 * spectra_here, 2 * LANES)
+                z = inner[pl.ds(k, 2)].reshape(2 * LANES, 2 * LANES)
                 made = lax.dot_general(
                     second[...], z, (((1,), (1,)), ((), ())), preferred_element_type=jnp.float32
                 ).astype(jnp.bfloat16)
                 for e in range(2):
-                    piece = made[:, e * spectra_here : (e + 1) * spectra_here]
-                    spec[i, :, k + e] = piece.reshape(owners, PACK, spectra_here)
+                    piece = made[:, e * LANES : (e + 1) * LANES]
+                    spec[i, :, k + e] = piece.reshape(owners, PACK, LANES)
                 return inside
 
             lax.fori_loop(0, per_group // 2, one_pair, 0)
@@ -240,12 +305,15 @@
 
         lax.fori_loop(0, GROUPS, second_stage, 0)
 
+    get_pick.wait()
     row = lax.broadcasted_iota(jnp.int32, (SUB, LANES), 0)
     col = lax.broadcasted_iota(jnp.int32, (SUB, LANES), 1)
     same = (lax.rem(col, SUB) == row).astype(jnp.float32) * (1.0 / (cores * spectra_here))
 
+    lower = lax.broadcasted_iota(jnp.int32, (SUB * inputs, LANES), 1) < spectra_chunk
+
     def correlate(group, carry):
-        for i in range(local_inputs):
+        for i in range(CHUNKS):
 
             def arrived(r, inside):
                 copy_in(i, group, lax.rem(me + r, owners)).wait_recv()
@@ -258,9 +326,15 @@
             k = group * per_group + n
             left, right = [], []
             for h in range(cores):
-                a = recv[h, :, k].astype(jnp.float32).reshape(inputs, 2, SUB, spectra_here)
-                re = a[:, 0].reshape(inputs * SUB, spectra_here)
-                im = a[:, 1].reshape(inputs * SUB, spectra_here)
+                a = recv[h, 0, :, k].astype(jnp.float32).reshape(inputs * SUB, LANES)
+                b = recv[h, 1, :, k].astype(jnp.float32).reshape(inputs * SUB, LANES)
+                one_in = jnp.where(lower, a, pltpu.roll(b, spectra_chunk, 1))
+                two_in = jnp.where(lower, pltpu.roll(a, spectra_chunk, 1), b)
+                one_in = one_in.reshape(stations, 2, SUB, LANES)
+                two_in = two_in.reshape(stations, 2, SUB, LANES)
+                both = jnp.stack([one_in, two_in], axis=1)
+                re = both[:, :, 0].reshape(inputs * SUB, LANES)
+                im = both[:, :, 1].reshape(inputs * SUB, LANES)
                 left.append(jnp.concatenate([re, im], axis=0).astype(jnp.bfloat16))
                 left.append(jnp.concatenate([im, -re], axis=0).astype(jnp.bfloat16))
                 right.append(re.astype(jnp.bfloat16))
@@ -292,10 +366,15 @@
         copy_out(i, group, lax.rem(me + 1 + r, owners)).wait_send()
         return carry
 
-    lax.fori_loop(0, local_inputs * GROUPS * (owners - 1), drain, 0)
-
-
-def kernel_fits(voltage, prototype, owners, inputs):
+    lax.fori_loop(0, CHUNKS * GROUPS * (owners - 1), drain, 0)
+
+    @pl.when(core < cores - 1)
+    def _():
+        halo.wait_send()
+
+
+def kernel_fits(voltage, prototype, stations, cores, inputs):
+    owners = stations * cores
     spectra_here = voltage.shape[2] // prototype.shape[1]
     channels = prototype.shape[1]
     return (
@@ -303,6 +382,8 @@
         and spectra_here == LANES
         and channels // owners == 32 * SUB
         and inputs * SUB == LANES
+        and inputs == 2 * stations
+        and cores == 2
     )
 
 
@@ -311,44 +392,48 @@
     tap_count, channels = prototype.shape
     stations, cores = lax.axis_size("stn"), lax.axis_size("chan")
     owners, inputs = stations * cores, stations * local_inputs
-    if not kernel_fits(voltage, prototype, owners, inputs):
+    if not kernel_fits(voltage, prototype, stations, cores, inputs):
         return general_shards(voltage, earlier_samples, prototype)
     spectra_here = samples // channels
     q_count = channels // LANES
     rows = channels // owners // q_count
-    tail = voltage[:, :, samples - (tap_count - 1) * channels :]
-    passed = passed_along(tail, "chan", 1)
-    history = jnp.where(lax.axis_index("chan") == 0, earlier_samples, passed)
-    stacked = jnp.concatenate(
-        [
-            history.reshape(components, local_inputs, tap_count - 1, q_count, LANES),
-            voltage.reshape(components, local_inputs, spectra_here, q_count, LANES),
-        ],
-        axis=2,
-    )
-    proto = prototype.reshape(tap_count, q_count, LANES)
-    consts = tables(channels, owners, rows, inputs)
+
+    def by_rows(array):
+        array = array.reshape(components, local_inputs, -1, LANES)
+        return jnp.transpose(array, (0, 2, 1, 3)).reshape(components, -1, LANES)
+
+    proto = jnp.repeat(prototype.reshape(tap_count, q_count, LANES), local_inputs, axis=1)
+    first, twist_cos, twist_sin, second, pick = tables(channels, owners, rows, inputs)
     vmem = pl.BlockSpec(memory_space=pltpu.VMEM)
-    blocks = spectra_here // SUB
+    anywhere = pl.BlockSpec(memory_space=pl.ANY)
+    frame_rows = local_inputs * q_count
+    blocks = spectra_here // CHUNKS // SUB
     made = pl.pallas_call(
         functools.partial(correlator, stations, cores),
         out_shape=jax.ShapeDtypeStruct((components, q_count, rows, inputs * inputs), jnp.float32),
-        in_specs=[vmem] * 7,
+        in_specs=[anywhere] * 4 + [vmem] * 4,
         out_specs=vmem,
         scratch_shapes=[
-            pltpu.VMEM((blocks, SUB, components, q_count, LANES), jnp.bfloat16),
-            pltpu.VMEM((q_count, spectra_here, 2 * LANES), jnp.bfloat16),
-            pltpu.VMEM((local_inputs, owners, q_count, PACK, spectra_here), jnp.bfloat16),
-            pltpu.VMEM((cores, inputs, q_count, PACK, spectra_here), jnp.bfloat16),
+            pltpu.VMEM((components, (spectra_here + tap_count - 1) * frame_rows, LANES), jnp.bfloat16),
+            pltpu.VMEM(first.shape, jnp.bfloat16),
+            pltpu.VMEM(pick.shape, jnp.bfloat16),
+            pltpu.VMEM((blocks, SUB, components, frame_rows, LANES), jnp.bfloat16),
+            pltpu.VMEM((q_count, LANES, 2 * LANES), jnp.bfloat16),
+            pltpu.VMEM((CHUNKS, owners, q_count, PACK, LANES), jnp.bfloat16),
+            pltpu.VMEM((cores, CHUNKS, stations, q_count, PACK, LANES), jnp.bfloat16),
             pltpu.VMEM((components, q_count // GROUPS, SUB, inputs * LANES), jnp.float32),
-            pltpu.SemaphoreType.DMA((local_inputs, GROUPS, owners)),
-            pltpu.SemaphoreType.DMA((local_inputs, GROUPS, owners)),
-            pltpu.SemaphoreType.DMA((local_inputs, GROUPS)),
+            pltpu.SemaphoreType.DMA((CHUNKS, GROUPS, owners)),
+            pltpu.SemaphoreType.DMA((CHUNKS, GROUPS, owners)),
+            pltpu.SemaphoreType.DMA((CHUNKS, GROUPS)),
+            pltpu.SemaphoreType.DMA((7,)),
+            pltpu.SemaphoreType.DMA((2,)),
         ],
         compiler_params=pltpu.CompilerParams(
-            collective_id=0, has_side_effects=True, vmem_limit_bytes=48 * 1024 * 1024
+            collective_id=0, has_side_effects=True, vmem_limit_bytes=58 * 1024 * 1024
         ),
-    )(stacked, proto, *consts)
+    )(
+        by_rows(voltage), by_rows(earlier_samples), first, pick, proto, twist_cos, twist_sin, second
+    )
     made = jnp.transpose(made, (0, 2, 1, 3))
     return made.reshape(components, rows * q_count, inputs * inputs)
 

time: 129 us -> 120 us (0.930)
  other arithmetic: 5.34 us -> 0 us
  local copies, waits for them, and re-layouts: 8.98 us -> 3.97 us
  Pallas kernels: 112 us -> 116 us
  starting transfers between devices: 2.52 us -> 0 us
    reshape x2 -> x0, local copies, waits for them, and re-layouts: 6.52 us -> none  [the longest x1 6.1 us: shards(): voltage.reshape(components, local_inputs, spectra_here, q_count, LANES)]
    concatenate x1 -> x0, other arithmetic: 4.83 us -> none  [shards(): jnp.concatenate([history.reshape(components, local_inputs, tap_count - 1,...]
    pallas_call x1, Pallas kernels: 112 us -> 116 us  [shards(): pl.pallas_call(functools.partial(correlator, stations, cores), out_shape=...]
    ppermute x1 -> x0, starting transfers between devices: 2.52 us -> none  [passed_along(): return lax.ppermute(block, axis, route)]
    slice x1 -> x0, local copies, waits for them, and re-layouts: 1.41 us -> none  [shards(): tail = voltage[:, :, samples - (tap_count - 1) * channels:]]
  transfers between devices with their start and end apart: 1 -> 0, of which waited for: 0 -> 0; matrix products, arithmetic and copies ran while one was open for 5% -> 0% of each run, Pallas kernels for 0% -> 0%
where the time goes in v2:
time: 120 us
  Pallas kernels  116 us (97%)
  local copies, waits for them, and re-layouts  3.97 us (3%)
    pallas_call x1, Pallas kernels, shards(): pl.pallas_call(functools.partial(correlator, stations, cores), out_shape=...  116 us

profile of v2, /device:TPU:0, one launch (start us, length us, event | category | flops | bytes accessed | tf_op | source)
XLA Modules:
  0.0 120.0 jit_solution(12970306147557266275)
XLA Ops:
  0.0 1.0 copy.14
  1.0 1.0 broadcast_in_dim.3
  2.0 116.0 %shard_map.82 = f32[2,32,8,256]{3,2,1,0:T(8,128)} custom-call(bf16[2,8192,128]{2,1,0:T(8,128)(2,1)} %bitcast.15, bf16[2,960,128]{2,1,0:T(8,128)(2,1)} %bitcast.19, bf16[1024,1024]{1,0:T(8,128)(2,1)} %constant.10.clone.first_hbm, bf16[2048,256]{1,0:T(8,128)(2,1)} %constant.14.clone.pick_hbm, f32[16,64,128]{2,1,0:T(8,128)} %bitcast.16, ...), custom_call_target="tpu_custom_call" | custom-call | tf_op jit(solution)/shard_map/pallas_call | solution.py:411
  118.0 2.0 %copy.13 = f32[2,8,32,256]{3,2,1,0:T(8,128)} copy(f32[2,8,32,256]{3,1,2,0:T(8,128)} %bitcast.17) | data formatting | bytes 1048576 | tf_op jit(solution)/shard_map/transpose | solution.py:437

commit v3 on v2

--- a/solution.py
+++ b/solution.py
@@ -103,6 +103,7 @@
     eye = np.eye(SUB)
     both = np.eye(2)
     first = np.einsum("ckdq,st,ij->ickstdqj", one, eye, both)
+    first = first.reshape(2, 2, GROUPS, q_count // GROUPS, SUB, -1).transpose(2, 0, 1, 3, 4, 5)
     first = first.reshape(4 * q_count * SUB, 4 * q_count * SUB)
     ang = 2.0 * np.pi * (np.outer(q, lane) % channels) / channels
     twist_cos, twist_sin = np.cos(ang), np.sin(ang)
@@ -125,8 +126,8 @@
 
 
 def correlator(
-    stations, cores, voltage, earlier, first_hbm, pick_hbm, proto, twist_cos, twist_sin, second, out,
-    stream, first, pick, held, inner, spec, recv, panel, send_sem, recv_sem, own_sem, load_sem, halo_sem,
+    stations, cores, voltage, earlier, first_hbm, pick_hbm, coeffs, twist_cos, twist_sin, second, out,
+    proto, stream, first, pick, held, inner, spec, recv, panel, send_sem, recv_sem, own_sem, load_sem, halo_sem,
 ):
     owners = stations * cores
     local_inputs = 2
@@ -186,6 +187,11 @@
         get_earlier.start()
 
     get_pick.start()
+
+    for q in range(q_count):
+        column = coeffs[:, q * LANES : (q + 1) * LANES]
+        for i in range(local_inputs):
+            proto[:, q * local_inputs + i, :] = column
 
     def copy_out(i, group, peer):
         part = pl.ds(group * per_group, per_group)
@@ -258,28 +264,31 @@
             def _():
                 halo.start()
 
-        half = 2 * q_count * SUB
-
-        def first_stage(n, carry):
-            pair, part = n // local_inputs, lax.rem(n, local_inputs)
-            wide = SUB * 2 * frame_rows
-            x = jnp.concatenate(
-                [held[2 * pair].reshape(wide, LANES), held[2 * pair + 1].reshape(wide, LANES)], axis=1
-            )
-            weights = first[pl.ds(pl.multiple_of(part * half, half), half), :]
-            g = jnp.dot(weights, x, preferred_element_type=jnp.float32)
-            g = g.reshape(2, q_count, SUB, 2 * LANES)
-            g = jnp.concatenate([g[..., :LANES], g[..., LANES:]], axis=2)
-            cos = twist_cos[...][:, None, :]
-            sin = twist_sin[...][:, None, :]
-            rows = pl.ds(pl.multiple_of(part * spectra_chunk + pair * PACK, PACK), PACK)
-            inner[:, rows, pl.ds(0, LANES)] = (g[0] * cos + g[1] * sin).astype(jnp.bfloat16)
-            inner[:, rows, pl.ds(LANES, LANES)] = (g[1] * cos - g[0] * sin).astype(jnp.bfloat16)
-            return carry
-
-        lax.fori_loop(0, blocks // 2 * local_inputs, first_stage, 0)
+        count = 4 * per_group * SUB
 
         def second_stage(group, carry):
+            ks = pl.ds(pl.multiple_of(group * per_group, per_group), per_group)
+
+            def first_stage(pair, inside):
+                wide = SUB * 2 * frame_rows
+                x = jnp.concatenate(
+                    [held[2 * pair].reshape(wide, LANES), held[2 * pair + 1].reshape(wide, LANES)], axis=1
+                )
+                weights = first[pl.ds(pl.multiple_of(group * count, count), count), :]
+                g = jnp.dot(weights, x, preferred_element_type=jnp.float32)
+                g = g.reshape(local_inputs, 2, per_group, SUB, 2 * LANES)
+                g = jnp.concatenate([g[..., :LANES], g[..., LANES:]], axis=3)
+                cos = twist_cos[ks, :][:, None, :]
+                sin = twist_sin[ks, :][:, None, :]
+                for part in range(local_inputs):
+                    re, im = g[part, 0], g[part, 1]
+                    rows = pl.ds(pl.multiple_of(part * spectra_chunk + pair * PACK, PACK), PACK)
+                    inner[ks, rows, pl.ds(0, LANES)] = (re * cos + im * sin).astype(jnp.bfloat16)
+                    inner[ks, rows, pl.ds(LANES, LANES)] = (im * cos - re * sin).astype(jnp.bfloat16)
+                return inside
+
+            lax.fori_loop(0, blocks // 2, first_stage, 0)
+
             def one_pair(n, inside):
                 k = group * per_group + 2 * n
                 z = inner[pl.ds(k, 2)].reshape(2 * LANES, 2 * LANES)
@@ -356,7 +365,8 @@
             low, pick[...], preferred_element_type=jnp.float32
         )
         total = total.reshape(2, per_group, SUB, inputs * inputs)
-        out[:, pl.ds(group * per_group, per_group)] = total
+        places = pl.ds(pl.multiple_of(group * per_group, per_group), per_group)
+        out[:, :, places, :] = jnp.swapaxes(total, 1, 2)
         return carry
 
     lax.fori_loop(0, GROUPS, correlate, 0)
@@ -402,7 +412,6 @@
         array = array.reshape(components, local_inputs, -1, LANES)
         return jnp.transpose(array, (0, 2, 1, 3)).reshape(components, -1, LANES)
 
-    proto = jnp.repeat(prototype.reshape(tap_count, q_count, LANES), local_inputs, axis=1)
     first, twist_cos, twist_sin, second, pick = tables(channels, owners, rows, inputs)
     vmem = pl.BlockSpec(memory_space=pltpu.VMEM)
     anywhere = pl.BlockSpec(memory_space=pl.ANY)
@@ -410,10 +419,11 @@
     blocks = spectra_here // CHUNKS // SUB
     made = pl.pallas_call(
         functools.partial(correlator, stations, cores),
-        out_shape=jax.ShapeDtypeStruct((components, q_count, rows, inputs * inputs), jnp.float32),
+        out_shape=jax.ShapeDtypeStruct((components, rows, q_count, inputs * inputs), jnp.float32),
         in_specs=[anywhere] * 4 + [vmem] * 4,
         out_specs=vmem,
         scratch_shapes=[
+            pltpu.VMEM((tap_count, frame_rows, LANES), jnp.float32),
             pltpu.VMEM((components, (spectra_here + tap_count - 1) * frame_rows, LANES), jnp.bfloat16),
             pltpu.VMEM(first.shape, jnp.bfloat16),
             pltpu.VMEM(pick.shape, jnp.bfloat16),
@@ -432,9 +442,8 @@
             collective_id=0, has_side_effects=True, vmem_limit_bytes=58 * 1024 * 1024
         ),
     )(
-        by_rows(voltage), by_rows(earlier_samples), first, pick, proto, twist_cos, twist_sin, second
-    )
-    made = jnp.transpose(made, (0, 2, 1, 3))
+        by_rows(voltage), by_rows(earlier_samples), first, pick, prototype, twist_cos, twist_sin, second
+    )
     return made.reshape(components, rows * q_count, inputs * inputs)
 
 

time: 120 us -> 115 us (0.958)
  Pallas kernels: 116 us -> 113 us
  local copies, waits for them, and re-layouts: 3.97 us -> 1.87 us
    pallas_call x1, Pallas kernels: 116 us -> 113 us  [shards(): pl.pallas_call(functools.partial(correlator, stations, cores), out_shape=...]
    transpose x1 -> x0, local copies, waits for them, and re-layouts: 1.99 us -> none  [shards(): made = jnp.transpose(made, (0, 2, 1, 3))]
where the time goes in v3:
time: 115 us
  Pallas kernels  113 us (98%)
  local copies, waits for them, and re-layouts  1.87 us (2%)
    pallas_call x1, Pallas kernels, shards(): pl.pallas_call(functools.partial(correlator, stations, cores), out_shape=...  113 us

profile of v3, /device:TPU:0, one launch (start us, length us, event | category | flops | bytes accessed | tf_op | source)
XLA Modules:
  0.0 115.2 jit_solution(11543120760639334434)
XLA Ops:
  0.0 113.3 %shard_map.82 = f32[2,8,32,256]{3,2,1,0:T(8,128)} custom-call(bf16[2,8192,128]{2,1,0:T(8,128)(2,1)} %bitcast.11, bf16[2,960,128]{2,1,0:T(8,128)(2,1)} %bitcast.13, bf16[1024,1024]{1,0:T(8,128)(2,1)} %constant.10.clone.first_hbm, bf16[2048,256]{1,0:T(8,128)(2,1)} %constant.14.clone.pick_hbm, f32[16,4096]{1,0:T(8,128)} %coeffs.1, ...), custom_call_target="tpu_custom_call" | custom-call | tf_op jit(solution)/shard_map/pallas_call | solution.py:420
  113.3 1.9 %copy.12 = f32[2,256,256]{2,1,0:T(8,128)} copy(f32[2,256,256]{2,1,0:T(8,128)} %bitcast.12) | data formatting | bytes 1048576
